TPU v7x, 512 devices: a whole 4x8x8 slice. The times are simulated.
512 devices in a mesh: row: 64 (over z, x, core), chan: 8 (over y).
Axes of the slice: x: 4, y: 8, z: 8, core: 2. Of those that a mesh axis runs over, the one named last changes fastest.
Arguments:
- slide: bfloat16 [256, 512, 256], P('chan', 'row'), may hold values from -6 to 6
- kernel_taps: float32 [256, 31, 31], P('chan'), may hold values from -0.1875 to 0.1875
- w_in: bfloat16 [1024, 256], replicated, may hold values from -0.375 to 0.375
- w_out: bfloat16 [256, 1024], replicated, may hold values from -0.1875 to 0.1875
Outputs:
- block_out: bfloat16 [256, 512, 256], P('chan', 'row')
All inputs are finite; a program needn't handle non-finite values.
Results may differ from a plain program's by a relative error of at most 0.0049.
Values may be sent and summed in bfloat16 or wider, within the bound.
A program may use at most 64 MiB of HBM per device.

v0:
```python
import functools

import jax
import jax.numpy as jnp
from jax import lax
from jax.experimental import pallas as pl
from jax.experimental.pallas import tpu as pltpu
from jax.sharding import PartitionSpec as P

MESH = pl.DeviceIdType.MESH
F32 = jnp.float32
BF16 = jnp.bfloat16

TAPS = 31
STEP = 5
SPAN = 7
CH = 16
ROWS = 16
WIN = 48
GROUPS = 2
GCH = CH // GROUPS
PARTS = 4
PCH = CH // PARTS
HALVES = 2


def iota(shape, dim):
    return lax.broadcasted_iota(jnp.int32, shape, dim)


def kernel(
    chips,
    chans,
    slide,
    taps,
    w_in,
    w_out,
    out,
    xbuf,
    tbuf,
    toep,
    win_v,
    wout_v,
    mbuf,
    sbuf,
    rbuf,
    obuf,
    send1,
    recv1,
    send2,
    recv2,
    send3,
    recv3,
    loc,
):
    row = lax.axis_index("row")
    y = lax.axis_index("chan")
    chip = row // 2
    k = row % 2
    m = y * 2 + k
    peers = 2 * chans

    barrier = pltpu.get_barrier_semaphore()

    def greet(r, c):
        pl.semaphore_signal(barrier, inc=1, device_id=(r, c), device_id_type=MESH)

    for dq in (1, chips - 1):
        for tk in range(2):
            greet((chip + dq) % chips * 2 + tk, y)
    for d in range(1, peers):
        t = (m + d) % peers
        greet(chip * 2 + t % 2, t // 2)

    taps_copy = pltpu.make_async_copy(taps.at[pl.ds(k * CH, CH)], tbuf, loc.at[0])
    taps_copy.start()
    own_copy = pltpu.make_async_copy(slide.at[pl.ds(k * CH, CH)], xbuf.at[2 + k], loc.at[1])
    own_copy.start()
    win_copy = pltpu.make_async_copy(w_in, win_v, loc.at[2])
    win_copy.start()
    wout_copy = pltpu.make_async_copy(w_out, wout_v, loc.at[3])
    wout_copy.start()

    pl.semaphore_wait(barrier, 4 + peers - 1)

    halo = []
    for p in range(PARTS):
        for dq in (1, -1, 0):
            for tk in range(2) if dq else (None,):
                core = 1 - k if tk is None else tk
                first = core * CH + p * PCH
                copy = pltpu.make_async_remote_copy(
                    src_ref=slide.at[pl.ds(first, PCH)],
                    dst_ref=xbuf.at[(1 - dq) * 2 + k, pl.ds(p * PCH, PCH)],
                    send_sem=send1.at[p, 2 if tk is None else (1 - dq) * 2 + tk],
                    recv_sem=recv1.at[p, (1 - dq) * 2 + k],
                    device_id=((chip + dq + chips) % chips * 2 + core, y),
                    device_id_type=MESH,
                )
                copy.start()
                halo.append(copy)

    taps_copy.wait()
    lane = iota((TAPS, 256), 1)
    spread = (lane % WIN == iota((TAPS, 256), 0)) & (lane < STEP * WIN)
    spread = spread.astype(BF16)
    keep = lane // WIN == iota((TAPS, 256), 0) % STEP
    pick = (iota((SPAN * ROWS, TAPS), 0) // ROWS == iota((SPAN * ROWS, TAPS), 1) // STEP).astype(BF16)
    for c in range(CH):
        wide = lax.dot_general(
            tbuf[c].astype(BF16), spread, (((0,), (0,)), ((), ())), preferred_element_type=F32
        )
        wide = jnp.where(keep, wide, 0.0).astype(BF16)
        base = jnp.dot(pick, wide, preferred_element_type=F32)
        for b in range(SPAN):
            band = pltpu.roll(base[b * ROWS : (b + 1) * ROWS], 1, 1, stride=1, stride_axis=0)
            toep[c, pl.ds(b * ROWS, ROWS), :] = band.astype(BF16)

    own_copy.wait()
    zeros = jnp.zeros((256 - STEP * WIN, 256), BF16)
    exchange = []
    for g in range(GROUPS):
        for p in range(g * PARTS // GROUPS, (g + 1) * PARTS // GROUPS):
            for slot in (0, 1, 4, 5, 3 - k):
                part = xbuf.at[slot, pl.ds(p * PCH, PCH)]
                pltpu.make_async_copy(part, part, recv1.at[p, slot]).wait()
            for c in range(p * PCH, (p + 1) * PCH):
                x = jnp.concatenate([xbuf[j, c].astype(F32) for j in range(6)], axis=0)
                cols = [x.astype(BF16)]
                for b in range(1, STEP):
                    cols.append(pltpu.roll(x, 256 - b, 1).astype(BF16))
                prod = jnp.dot(toep[c], jnp.concatenate(cols + [zeros], axis=0), preferred_element_type=F32)
                total = x[ROWS : 2 * ROWS]
                for b in range(SPAN):
                    piece = prod[b * ROWS : (b + 1) * ROWS]
                    shift = (TAPS // 2 - STEP * b) % 256
                    total = total + (pltpu.roll(piece, shift, 1) if shift else piece)
                mbuf[c] = total
        mixed = mbuf[pl.ds(g * GCH, GCH)]
        sbuf[g] = jnp.swapaxes(mixed, 0, 1).astype(BF16)
        for d in range(1, peers):
            t = (m + d) % peers
            copy = pltpu.make_async_remote_copy(
                src_ref=sbuf.at[g, t % 2 * chans + t // 2],
                dst_ref=rbuf.at[g, m],
                send_sem=send2.at[g, d],
                recv_sem=recv2.at[g, m],
                device_id=(chip * 2 + t % 2, t // 2),
                device_id_type=MESH,
            )
            copy.start()
            exchange.append(copy)
        rbuf[g, m] = sbuf[g, k * chans + y]

    win_copy.wait()
    wout_copy.wait()
    for g in range(GROUPS):
        for d in range(1, peers):
            part = rbuf.at[g, (m + d) % peers]
            pltpu.make_async_copy(part, part, recv2.at[g, (m + d) % peers]).wait()
    wide = 256 // HALVES
    back = []
    for half in range(HALVES):
        px = pl.ds(half * wide, wide)
        inner = jnp.concatenate(
            [rbuf[g, s, :, px].astype(F32) for s in range(peers) for g in range(GROUPS)], axis=0
        )
        flat = inner.astype(BF16)
        branch = jnp.zeros((256, wide), F32)
        for f in range(4):
            v = jnp.dot(win_v[pl.ds(f * 256, 256), :], flat, preferred_element_type=F32)
            hidden = (v * (1.0 + lax.erf(v * (0.5**0.5))) * 0.5).astype(BF16)
            branch = branch + jnp.dot(wout_v[:, pl.ds(f * 256, 256)], hidden, preferred_element_type=F32)
        branch = branch.astype(BF16).astype(F32)
        obuf[half] = (inner + branch).astype(BF16)
        depth = 2 * CH
        for d in range(1, chans):
            t = (y + d) % chans
            copy = pltpu.make_async_remote_copy(
                src_ref=obuf.at[half, pl.ds(t * depth, depth)],
                dst_ref=out.at[half, y],
                send_sem=send3.at[half, d],
                recv_sem=recv3.at[half, y],
                device_id=(row, t),
                device_id_type=MESH,
            )
            copy.start()
            back.append(copy)
        out[half, y] = obuf[half, pl.ds(pl.multiple_of(y * depth, depth), depth), :]

    for copy in halo + exchange + back:
        copy.wait_send()
    for half in range(HALVES):
        for d in range(1, chans):
            part = out.at[half, (y + d) % chans]
            pltpu.make_async_copy(part, part, recv3.at[half, (y + d) % chans]).wait()


def solution(mesh):
    chips = mesh.shape["row"] // 2
    chans = mesh.shape["chan"]
    peers = 2 * chans
    placed = (P("chan", "row", None), P("chan", None, None), P(), P())

    def shards(slide, kernel_taps, w_in, w_out):
        depth, rows, width = slide.shape
        any_space = pl.BlockSpec(memory_space=pl.ANY)
        got = pl.pallas_call(
            functools.partial(kernel, chips, chans),
            out_shape=jax.ShapeDtypeStruct((HALVES, rows, depth, width // HALVES), BF16),
            in_specs=[any_space] * 4,
            out_specs=pl.BlockSpec(memory_space=pltpu.VMEM),
            scratch_shapes=[
                pltpu.VMEM((6, CH, rows, width), BF16),
                pltpu.VMEM((CH, TAPS, TAPS), F32),
                pltpu.VMEM((CH, SPAN * ROWS, 256), BF16),
                pltpu.VMEM(w_in.shape, BF16),
                pltpu.VMEM(w_out.shape, BF16),
                pltpu.VMEM((CH, ROWS, width), F32),
                pltpu.VMEM((GROUPS, ROWS, GCH, width), BF16),
                pltpu.VMEM((GROUPS, peers, GCH, width), BF16),
                pltpu.VMEM((HALVES, 256, width // HALVES), BF16),
                pltpu.SemaphoreType.DMA((PARTS, 6)),
                pltpu.SemaphoreType.DMA((PARTS, 6)),
                pltpu.SemaphoreType.DMA((GROUPS, peers)),
                pltpu.SemaphoreType.DMA((GROUPS, peers)),
                pltpu.SemaphoreType.DMA((HALVES, chans)),
                pltpu.SemaphoreType.DMA((HALVES, chans)),
                pltpu.SemaphoreType.DMA((4,)),
            ],
            compiler_params=pltpu.CompilerParams(
                collective_id=0, has_side_effects=True, vmem_limit_bytes=40 * 2**20
            ),
        )(slide, kernel_taps, w_in, w_out)
        return jnp.transpose(got, (2, 1, 0, 3)).reshape(slide.shape)

    return jax.shard_map(shards, mesh=mesh, in_specs=placed, out_specs=placed[0], check_vma=False)
```

profile of v0, /device:TPU:1, one launch (start us, length us, event | category | flops | bytes accessed | tf_op | source)
XLA Modules:
  0.0 39.9 jit_solution(10989201815565485729)
XLA Ops:
  0.0 0.0 copy-start
  0.0 0.0 copy-start.2
  0.0 1.4 %copy.6.taps = f32[32,31,31]{2,1,0:T(8,128)S(1)} copy(f32[32,31,31]{2,0,1:T(8,128)} %param.5) | data formatting | bytes 246016 | tf_op args[1]
  1.4 0.0 copy-done
  1.4 0.0 copy-done.2
  1.4 0.0 copy-start.1
  1.4 1.0 %copy-done.1 = bf16[256,1024]{1,0:T(8,128)(2,1)S(1)} copy-done((bf16[256,1024]{1,0:T(8,128)(2,1)S(1)}, bf16[256,1024]{1,0:T(8,128)(2,1)}, u32[]{:S(2)}) %copy-start.1) | copy-done | bytes 524312
  2.5 36.7 %shard_map.46 = bf16[2,8,32,128]{3,2,1,0:T(8,128)(2,1)S(1)} custom-call(bf16[32,8,256]{2,1,0:T(8,128)(2,1)S(1)} %copy-done.2, f32[32,31,31]{2,1,0:T(8,128)S(1)} %copy.6.taps, bf16[1024,256]{1,0:T(8,128)(2,1)S(1)} %copy-done, bf16[256,1024]{1,0:T(8,128)(2,1)S(1)} %copy-done.1), custom_call_target="tpu_custom_call" | custom-call | tf_op jit(solution)/shard_map/pallas_call | solution.py:208
  39.2 0.7 %copy.9 = bf16[32,8,2,128]{3,1,2,0:T(8,128)(2,1)} copy(bf16[32,8,2,128]{3,0,1,2:T(8,128)(2,1)S(1)} %bitcast.4) | data formatting | bytes 262144 | tf_op jit(solution)/shard_map/transpose | solution.py:235
Async XLA Ops:
  0.0 1.4 %copy-start = (bf16[1024,256]{1,0:T(8,128)(2,1)S(1)}, bf16[1024,256]{1,0:T(8,128)(2,1)}, u32[]{:S(2)}) copy-start(bf16[1024,256]{1,0:T(8,128)(2,1)} %w_in.1) | copy-start | bytes 1572868
  0.0 1.4 %copy-start.2 = (bf16[32,8,256]{2,1,0:T(8,128)(2,1)S(1)}, bf16[32,8,256]{2,1,0:T(8,128)(2,1)}, u32[]{:S(2)}) copy-start(bf16[32,8,256]{2,1,0:T(8,128)(2,1)} %slide.1) | copy-start | bytes 393220
  1.4 1.0 %copy-start.1 = (bf16[256,1024]{1,0:T(8,128)(2,1)S(1)}, bf16[256,1024]{1,0:T(8,128)(2,1)}, u32[]{:S(2)}) copy-start(bf16[256,1024]{1,0:T(8,128)(2,1)} %w_out.1) | copy-start | bytes 1572868
where the time goes:
time: 40.1 us; the launch traced here: 39.9 us
  Pallas kernels  36.7 us (92%)
  local copies, waits for them, and re-layouts  3.15 us (8%)
    pallas_call x1, Pallas kernels, shards(): pl.pallas_call(functools.partial(kernel, chips, chans), out_shape=jax.Sha...  36.7 us
    unnamed x7, local copies, waits for them, and re-layouts  2.44 us

commit v1 on v0

v1 whole, which is shorter than its diff:
```python
import functools

import jax
import jax.numpy as jnp
from jax import lax
from jax.experimental import pallas as pl
from jax.experimental.pallas import tpu as pltpu
from jax.sharding import PartitionSpec as P

MESH = pl.DeviceIdType.MESH
F32 = jnp.float32
BF16 = jnp.bfloat16

TAPS = 31
STEP = 5
SPAN = 7
CH = 16
ROWS = 16
WIN = 48
GROUPS = 2
GCH = CH // GROUPS
PARTS = 4
PCH = CH // PARTS


def iota(shape, dim):
    return lax.broadcasted_iota(jnp.int32, shape, dim)


def kernel(
    chips,
    chans,
    slide,
    taps,
    w_in,
    w_out,
    out,
    xbuf,
    tbuf,
    toep,
    win_v,
    wout_v,
    mbuf,
    sbuf,
    rbuf,
    obuf,
    send1,
    recv1,
    send2,
    recv2,
    send3,
    recv3,
    loc,
    ring2,
    ring4,
):
    row = lax.axis_index("row")
    y = lax.axis_index("chan")
    chip = row // 2
    k = row % 2
    m = y * 2 + k
    peers = 2 * chans
    last = chip == chips - 1

    barrier = pltpu.get_barrier_semaphore()

    def signal(sem, r, c):
        pl.semaphore_signal(sem, inc=1, device_id=(r, c), device_id_type=MESH)

    for dq in (1, chips - 1):
        for tk in range(2):
            signal(barrier, (chip + dq) % chips * 2 + tk, y)
    signal(barrier, chip * 2 + 1 - k, y)
    for dy in (1, chans - 1):
        for tk in range(2):
            signal(barrier, chip * 2 + tk, (y + dy) % chans)

    taps_copy = pltpu.make_async_copy(
        taps.at[:, pl.ds(pl.multiple_of(k * CH, CH), CH)], tbuf.at[pl.ds(0, TAPS)], loc.at[0]
    )
    own_copy = pltpu.make_async_copy(slide.at[pl.ds(k * CH, CH)], xbuf.at[2 + k], loc.at[1])
    win_copy = pltpu.make_async_copy(w_in, win_v, loc.at[2])
    wout_copy = pltpu.make_async_copy(w_out, wout_v, loc.at[3])
    for copy in (taps_copy, own_copy, win_copy, wout_copy):
        copy.start()

    def prepare():
        taps_copy.wait()
        tbuf[TAPS] = jnp.zeros(tbuf.shape[1:], F32)
        lane = iota((TAPS + 1, 256), 1)
        spread = (lane % WIN == iota((TAPS + 1, 256), 0)) & (lane < STEP * WIN)
        spread = spread.astype(BF16)
        keep = iota((TAPS, 256), 1) // WIN == iota((TAPS, 256), 0) % STEP
        pick = iota((SPAN * ROWS, TAPS), 0) // ROWS == iota((SPAN * ROWS, TAPS), 1) // STEP
        pick = pick.astype(BF16)
        plane = jnp.swapaxes(tbuf[...], 0, 1).astype(BF16)
        for c in range(CH):
            wide = lax.dot_general(plane[c], spread, (((0,), (0,)), ((), ())), preferred_element_type=F32)
            wide = jnp.where(keep, wide, 0.0).astype(BF16)
            base = jnp.dot(pick, wide, preferred_element_type=F32)
            for b in range(SPAN):
                band = pltpu.roll(base[b * ROWS : (b + 1) * ROWS], 1, 1, stride=1, stride_axis=0)
                toep[c, pl.ds(b * ROWS, ROWS), :] = band.astype(BF16)

    @pl.when(jnp.logical_not(last))
    def _():
        prepare()

    pl.semaphore_wait(barrier, 9)

    halo = []
    for dq in (1, -1, 0):
        for p in range(PARTS):
            for tk in range(2) if dq else (None,):
                core = 1 - k if tk is None else tk
                first = core * CH + p * PCH
                copy = pltpu.make_async_remote_copy(
                    src_ref=slide.at[pl.ds(first, PCH)],
                    dst_ref=xbuf.at[(1 - dq) * 2 + k, pl.ds(p * PCH, PCH)],
                    send_sem=send1.at[p, 2 if tk is None else (1 - dq) * 2 + tk],
                    recv_sem=recv1.at[p, (1 - dq) * 2 + k],
                    device_id=((chip + dq + chips) % chips * 2 + core, y),
                    device_id_type=MESH,
                )
                copy.start()
                halo.append(copy)

    @pl.when(last)
    def _():
        prepare()

    for dy in (1, chans - 1):
        signal(ring2, row, (y + dy) % chans)
    pl.semaphore_wait(ring2, 2)
    for dy in (2, chans - 2):
        signal(ring4, row, (y + dy) % chans)

    far = sorted(range(1, chans), key=lambda d: -min(d, chans - d))
    own_copy.wait()
    zeros = jnp.zeros((256 - STEP * WIN, 256), BF16)
    exchange = []
    for g in range(GROUPS):
        for p in range(g * PARTS // GROUPS, (g + 1) * PARTS // GROUPS):
            for slot in (0, 1, 4, 5, 3 - k):
                part = xbuf.at[slot, pl.ds(p * PCH, PCH)]
                pltpu.make_async_copy(part, part, recv1.at[p, slot]).wait()
            for c in range(p * PCH, (p + 1) * PCH):
                x = jnp.concatenate([xbuf[j, c].astype(F32) for j in range(6)], axis=0)
                cols = [x.astype(BF16)]
                for b in range(1, STEP):
                    cols.append(pltpu.roll(x, 256 - b, 1).astype(BF16))
                prod = jnp.dot(toep[c], jnp.concatenate(cols + [zeros], axis=0), preferred_element_type=F32)
                total = x[ROWS : 2 * ROWS]
                for b in range(SPAN):
                    piece = prod[b * ROWS : (b + 1) * ROWS]
                    shift = (TAPS // 2 - STEP * b) % 256
                    total = total + (pltpu.roll(piece, shift, 1) if shift else piece)
                mbuf[c] = total
        mixed = mbuf[pl.ds(g * GCH, GCH)]
        sbuf[g] = jnp.swapaxes(mixed, 0, 1).astype(BF16)
        if g == 0:
            pl.semaphore_wait(ring4, 2)
        for d in far + [0]:
            for tk in (0, 1) if d else (None,):
                core = 1 - k if tk is None else tk
                t = (y + d) % chans
                copy = pltpu.make_async_remote_copy(
                    src_ref=sbuf.at[g, core * chans + t],
                    dst_ref=rbuf.at[g, m],
                    send_sem=send2.at[g, 2 * d + (tk or 0)],
                    recv_sem=recv2.at[g, m],
                    device_id=(chip * 2 + core, t),
                    device_id_type=MESH,
                )
                copy.start()
                exchange.append(copy)
        rbuf[g, m] = sbuf[g, k * chans + y]

    win_copy.wait()
    wout_copy.wait()
    for g in range(GROUPS):
        for d in range(1, peers):
            part = rbuf.at[g, (m + d) % peers]
            pltpu.make_async_copy(part, part, recv2.at[g, (m + d) % peers]).wait()
    inner = jnp.concatenate([rbuf[g, s].astype(F32) for s in range(peers) for g in range(GROUPS)], axis=0)
    flat = inner.astype(BF16)
    branch = jnp.zeros((256, 256), F32)
    for f in range(4):
        v = jnp.dot(win_v[pl.ds(f * 256, 256), :], flat, preferred_element_type=F32)
        hidden = (v * (1.0 + lax.erf(v * (0.5**0.5))) * 0.5).astype(BF16)
        branch = branch + jnp.dot(wout_v[:, pl.ds(f * 256, 256)], hidden, preferred_element_type=F32)
    obuf[...] = (inner + branch.astype(BF16).astype(F32)).astype(BF16)
    back = []
    depth = 2 * CH
    for d in far:
        t = (y + d) % chans
        copy = pltpu.make_async_remote_copy(
            src_ref=obuf.at[pl.ds(pl.multiple_of(t * depth, depth), depth)],
            dst_ref=out.at[y],
            send_sem=send3.at[d],
            recv_sem=recv3.at[y],
            device_id=(row, t),
            device_id_type=MESH,
        )
        copy.start()
        back.append(copy)
    out[y] = obuf[pl.ds(pl.multiple_of(y * depth, depth), depth), :]

    for copy in halo + exchange + back:
        copy.wait_send()
    for d in range(1, chans):
        part = out.at[(y + d) % chans]
        pltpu.make_async_copy(part, part, recv3.at[(y + d) % chans]).wait()


def solution(mesh):
    chips = mesh.shape["row"] // 2
    chans = mesh.shape["chan"]
    peers = 2 * chans
    placed = (P("chan", "row", None), P("chan", None, None), P(), P())

    def shards(slide, kernel_taps, w_in, w_out):
        depth, rows, width = slide.shape
        hbm = pl.BlockSpec(memory_space=pltpu.HBM)
        got = pl.pallas_call(
            functools.partial(kernel, chips, chans),
            out_shape=jax.ShapeDtypeStruct((rows, depth, width), BF16),
            in_specs=[hbm] * 4,
            out_specs=pl.BlockSpec(memory_space=pltpu.VMEM),
            scratch_shapes=[
                pltpu.VMEM((6, CH, rows, width), BF16),
                pltpu.VMEM((TAPS + 1, CH, TAPS), F32),
                pltpu.VMEM((CH, SPAN * ROWS, 256), BF16),
                pltpu.VMEM(w_in.shape, BF16),
                pltpu.VMEM(w_out.shape, BF16),
                pltpu.VMEM((CH, ROWS, width), F32),
                pltpu.VMEM((GROUPS, ROWS, GCH, width), BF16),
                pltpu.VMEM((GROUPS, peers, GCH, width), BF16),
                pltpu.VMEM((256, width), BF16),
                pltpu.SemaphoreType.DMA((PARTS, 6)),
                pltpu.SemaphoreType.DMA((PARTS, 6)),
                pltpu.SemaphoreType.DMA((GROUPS, peers)),
                pltpu.SemaphoreType.DMA((GROUPS, peers)),
                pltpu.SemaphoreType.DMA((chans,)),
                pltpu.SemaphoreType.DMA((chans,)),
                pltpu.SemaphoreType.DMA((4,)),
                pltpu.SemaphoreType.REGULAR,
                pltpu.SemaphoreType.REGULAR,
            ],
            compiler_params=pltpu.CompilerParams(
                collective_id=0, has_side_effects=True, vmem_limit_bytes=60 * 2**20
            ),
        )(slide, jnp.transpose(kernel_taps, (1, 0, 2)), w_in, w_out)
        return jnp.transpose(got, (1, 0, 2))

    return jax.shard_map(shards, mesh=mesh, in_specs=placed, out_specs=placed[0], check_vma=False)
```

time: 40.1 us -> 35.9 us (0.90)
  Pallas kernels: 36.7 us -> 34.1 us
  local copies, waits for them, and re-layouts: 3.15 us -> 1.64 us
    pallas_call x1, Pallas kernels: 36.7 us -> 34.1 us  [shards(): pl.pallas_call(functools.partial(kernel, chips, chans), out_shape=jax.Sha...]
    unnamed x7 -> x0, local copies, waits for them, and re-layouts: 2.44 us -> none
    transpose x1, local copies, waits for them, and re-layouts: 0.71 us -> 1.64 us  [shards(): return jnp.transpose(got, (1, 0, 2))]
where the time goes in v1:
time: 35.9 us; the launch traced here: 35.8 us
  Pallas kernels  34.1 us (95%)
  local copies, waits for them, and re-layouts  1.64 us (5%)
    pallas_call x1, Pallas kernels, shards(): pl.pallas_call(functools.partial(kernel, chips, chans), out_shape=jax.Sha...  34.1 us
    transpose x1, local copies, waits for them, and re-layouts, shards(): return jnp.transpose(got, (1, 0, 2))  1.64 us

profile of v1, /device:TPU:1, one launch (start us, length us, event | category | flops | bytes accessed | tf_op | source)
XLA Modules:
  0.0 35.8 jit_solution(3903637423945620440)
XLA Ops:
  0.0 34.1 %shard_map.46 = bf16[8,32,256]{2,1,0:T(8,128)(2,1)} custom-call(bf16[32,8,256]{2,1,0:T(8,128)(2,1)} %slide.1, f32[31,32,31]{2,1,0:T(8,128)} %bitcast.3, bf16[1024,256]{1,0:T(8,128)(2,1)} %w_in.1, bf16[256,1024]{1,0:T(8,128)(2,1)} %w_out.1), custom_call_target="tpu_custom_call" | custom-call | tf_op jit(solution)/shard_map/pallas_call | solution.py:225
  34.1 1.6 %copy.5 = bf16[32,8,256]{2,1,0:T(8,128)(2,1)} copy(bf16[32,8,256]{2,0,1:T(8,128)(2,1)} %bitcast.2) | data formatting | bytes 262144 | tf_op jit(solution)/shard_map/transpose | solution.py:254

commit v2 on v1

--- a/solution.py
+++ b/solution.py
@@ -51,8 +51,7 @@
     send3,
     recv3,
     loc,
-    ring2,
-    ring4,
+    back_x,
 ):
     row = lax.axis_index("row")
     y = lax.axis_index("chan")
@@ -61,19 +60,20 @@
     m = y * 2 + k
     peers = 2 * chans
     last = chip == chips - 1
-
-    barrier = pltpu.get_barrier_semaphore()
+    below = (chip + 1) % chips
+    above = (chip + chips - 1) % chips
 
     def signal(sem, r, c):
         pl.semaphore_signal(sem, inc=1, device_id=(r, c), device_id_type=MESH)
 
-    for dq in (1, chips - 1):
+    barrier = pltpu.get_barrier_semaphore()
+    for tk in range(2):
+        signal(barrier, above * 2 + tk, y)
+    signal(barrier, chip * 2 + 1 - k, y)
+    base = jnp.where(last, above, chip)
+    for d in range(1, chans):
         for tk in range(2):
-            signal(barrier, (chip + dq) % chips * 2 + tk, y)
-    signal(barrier, chip * 2 + 1 - k, y)
-    for dy in (1, chans - 1):
-        for tk in range(2):
-            signal(barrier, chip * 2 + tk, (y + dy) % chans)
+            signal(barrier, base * 2 + tk, (y + d) % chans)
 
     taps_copy = pltpu.make_async_copy(
         taps.at[:, pl.ds(pl.multiple_of(k * CH, CH), CH)], tbuf.at[pl.ds(0, TAPS)], loc.at[0]
@@ -106,10 +106,14 @@
     def _():
         prepare()
 
-    pl.semaphore_wait(barrier, 9)
+    pl.semaphore_wait(barrier, jnp.where(last, 3, jnp.where(chip == chips - 2, 2 * peers - 1, peers + 1)))
+
+    for tk in range(2):
+        signal(back_x, below * 2 + tk, y)
 
     halo = []
-    for dq in (1, -1, 0):
+
+    def send_rows(dq):
         for p in range(PARTS):
             for tk in range(2) if dq else (None,):
                 core = 1 - k if tk is None else tk
@@ -119,21 +123,21 @@
                     dst_ref=xbuf.at[(1 - dq) * 2 + k, pl.ds(p * PCH, PCH)],
                     send_sem=send1.at[p, 2 if tk is None else (1 - dq) * 2 + tk],
                     recv_sem=recv1.at[p, (1 - dq) * 2 + k],
-                    device_id=((chip + dq + chips) % chips * 2 + core, y),
+                    device_id=({1: below, 0: chip, -1: above}[dq] * 2 + core, y),
                     device_id_type=MESH,
                 )
                 copy.start()
                 halo.append(copy)
 
+    send_rows(1)
+    send_rows(0)
+
+    pl.semaphore_wait(back_x, 2)
+    send_rows(-1)
+
     @pl.when(last)
     def _():
         prepare()
-
-    for dy in (1, chans - 1):
-        signal(ring2, row, (y + dy) % chans)
-    pl.semaphore_wait(ring2, 2)
-    for dy in (2, chans - 2):
-        signal(ring4, row, (y + dy) % chans)
 
     far = sorted(range(1, chans), key=lambda d: -min(d, chans - d))
     own_copy.wait()
@@ -148,7 +152,7 @@
                 x = jnp.concatenate([xbuf[j, c].astype(F32) for j in range(6)], axis=0)
                 cols = [x.astype(BF16)]
                 for b in range(1, STEP):
-                    cols.append(pltpu.roll(x, 256 - b, 1).astype(BF16))
+                    cols.append(pltpu.roll(cols[0], 256 - b, 1))
                 prod = jnp.dot(toep[c], jnp.concatenate(cols + [zeros], axis=0), preferred_element_type=F32)
                 total = x[ROWS : 2 * ROWS]
                 for b in range(SPAN):
@@ -158,8 +162,6 @@
                 mbuf[c] = total
         mixed = mbuf[pl.ds(g * GCH, GCH)]
         sbuf[g] = jnp.swapaxes(mixed, 0, 1).astype(BF16)
-        if g == 0:
-            pl.semaphore_wait(ring4, 2)
         for d in far + [0]:
             for tk in (0, 1) if d else (None,):
                 core = 1 - k if tk is None else tk
@@ -189,27 +191,31 @@
         v = jnp.dot(win_v[pl.ds(f * 256, 256), :], flat, preferred_element_type=F32)
         hidden = (v * (1.0 + lax.erf(v * (0.5**0.5))) * 0.5).astype(BF16)
         branch = branch + jnp.dot(wout_v[:, pl.ds(f * 256, 256)], hidden, preferred_element_type=F32)
-    obuf[...] = (inner + branch.astype(BF16).astype(F32)).astype(BF16)
+    result = (inner + branch.astype(BF16).astype(F32)).astype(BF16)
+    obuf[0] = result[:, :128]
+    obuf[1] = result[:, 128:]
+    depth = 2 * CH
+    targets = sorted(range(chans), key=lambda t: min(t, chans - t))
     back = []
-    depth = 2 * CH
-    for d in far:
-        t = (y + d) % chans
+    for t in targets:
         copy = pltpu.make_async_remote_copy(
-            src_ref=obuf.at[pl.ds(pl.multiple_of(t * depth, depth), depth)],
-            dst_ref=out.at[y],
-            send_sem=send3.at[d],
+            src_ref=obuf.at[:, pl.ds(t * depth, depth)],
+            dst_ref=out.at[:, y],
+            send_sem=send3.at[t],
             recv_sem=recv3.at[y],
             device_id=(row, t),
             device_id_type=MESH,
         )
-        copy.start()
+        pl.when(y != t)(copy.start)
         back.append(copy)
-    out[y] = obuf[pl.ds(pl.multiple_of(y * depth, depth), depth), :]
-
-    for copy in halo + exchange + back:
+    out[:, y] = obuf[:, pl.ds(pl.multiple_of(y * depth, depth), depth), :]
+
+    for copy in halo + exchange:
         copy.wait_send()
+    for t, copy in zip(targets, back):
+        pl.when(y != t)(copy.wait_send)
     for d in range(1, chans):
-        part = out.at[(y + d) % chans]
+        part = out.at[:, (y + d) % chans]
         pltpu.make_async_copy(part, part, recv3.at[(y + d) % chans]).wait()
 
 
@@ -224,7 +230,7 @@
         hbm = pl.BlockSpec(memory_space=pltpu.HBM)
         got = pl.pallas_call(
             functools.partial(kernel, chips, chans),
-            out_shape=jax.ShapeDtypeStruct((rows, depth, width), BF16),
+            out_shape=jax.ShapeDtypeStruct((2, rows, depth, width // 2), BF16),
             in_specs=[hbm] * 4,
             out_specs=pl.BlockSpec(memory_space=pltpu.VMEM),
             scratch_shapes=[
@@ -236,7 +242,7 @@
                 pltpu.VMEM((CH, ROWS, width), F32),
                 pltpu.VMEM((GROUPS, ROWS, GCH, width), BF16),
                 pltpu.VMEM((GROUPS, peers, GCH, width), BF16),
-                pltpu.VMEM((256, width), BF16),
+                pltpu.VMEM((2, 256, width // 2), BF16),
                 pltpu.SemaphoreType.DMA((PARTS, 6)),
                 pltpu.SemaphoreType.DMA((PARTS, 6)),
                 pltpu.SemaphoreType.DMA((GROUPS, peers)),
@@ -245,12 +251,11 @@
                 pltpu.SemaphoreType.DMA((chans,)),
                 pltpu.SemaphoreType.DMA((4,)),
                 pltpu.SemaphoreType.REGULAR,
-                pltpu.SemaphoreType.REGULAR,
             ],
             compiler_params=pltpu.CompilerParams(
                 collective_id=0, has_side_effects=True, vmem_limit_bytes=60 * 2**20
             ),
         )(slide, jnp.transpose(kernel_taps, (1, 0, 2)), w_in, w_out)
-        return jnp.transpose(got, (1, 0, 2))
+        return jnp.transpose(got, (2, 1, 0, 3)).reshape(slide.shape)
 
     return jax.shard_map(shards, mesh=mesh, in_specs=placed, out_specs=placed[0], check_vma=False)

time: 35.9 us -> 33.2 us (0.925)
  the two profiles are of different devices: /device:TPU:1 before, /device:TPU:16 now
where the time goes in v2:
time: 33.2 us; the launch traced here: 33.1 us
  Pallas kernels  31.4 us (95%)
  local copies, waits for them, and re-layouts  1.61 us (5%)
    pallas_call x1, Pallas kernels, shards(): pl.pallas_call(functools.partial(kernel, chips, chans), out_shape=jax.Sha...  31.4 us
    transpose x1, local copies, waits for them, and re-layouts, shards(): return jnp.transpose(got, (2, 1, 0, 3)).reshape(slide.shape)  1.61 us

profile of v2, /device:TPU:16, one launch (start us, length us, event | category | flops | bytes accessed | tf_op | source)
XLA Modules:
  0.0 33.1 jit_solution(467212473977531342)
XLA Ops:
  0.0 31.4 %shard_map.46 = bf16[2,8,32,128]{3,2,1,0:T(8,128)(2,1)} custom-call(bf16[32,8,256]{2,1,0:T(8,128)(2,1)} %slide.1, f32[31,32,31]{2,1,0:T(8,128)} %bitcast.6, bf16[1024,256]{1,0:T(8,128)(2,1)} %w_in.1, bf16[256,1024]{1,0:T(8,128)(2,1)} %w_out.1), custom_call_target="tpu_custom_call" | custom-call | tf_op jit(solution)/shard_map/pallas_call | solution.py:231
  31.4 1.6 %copy.7 = bf16[32,8,2,128]{3,1,2,0:T(8,128)(2,1)} copy(bf16[32,8,2,128]{3,0,1,2:T(8,128)(2,1)} %bitcast.5) | data formatting | bytes 262144 | tf_op jit(solution)/shard_map/transpose | solution.py:259

commit v3 on v2

--- a/solution.py
+++ b/solution.py
@@ -69,11 +69,42 @@
     barrier = pltpu.get_barrier_semaphore()
     for tk in range(2):
         signal(barrier, above * 2 + tk, y)
-    signal(barrier, chip * 2 + 1 - k, y)
+
+    def row_copy(dq, p, tk):
+        core = 1 - k if dq == 0 else tk
+        first = core * CH + p * PCH
+        return pltpu.make_async_remote_copy(
+            src_ref=slide.at[pl.ds(first, PCH)],
+            dst_ref=xbuf.at[(1 - dq) * 2 + k, pl.ds(p * PCH, PCH)],
+            send_sem=send1.at[p, (1 - dq) * 2 + tk],
+            recv_sem=recv1.at[p, (1 - dq) * 2 + k],
+            device_id=({1: below, 0: chip, -1: above}[dq] * 2 + core, y),
+            device_id_type=MESH,
+        )
+
+    def send_rows(dq):
+        for p in range(PARTS):
+            for tk in range(2 if dq else 1):
+                row_copy(dq, p, tk).start()
+
+    @pl.when(last)
+    def _():
+        pl.semaphore_wait(barrier, 2)
+        send_rows(1)
+
     base = jnp.where(last, above, chip)
     for d in range(1, chans):
         for tk in range(2):
             signal(barrier, base * 2 + tk, (y + d) % chans)
+
+    @pl.when(jnp.logical_not(last))
+    def _():
+        signal(barrier, chip * 2 + 1 - k, y)
+
+    @pl.when(chip < chips - 2)
+    def _():
+        for tk in range(2):
+            signal(barrier, below * 2 + tk, y)
 
     taps_copy = pltpu.make_async_copy(
         taps.at[:, pl.ds(pl.multiple_of(k * CH, CH), CH)], tbuf.at[pl.ds(0, TAPS)], loc.at[0]
@@ -105,34 +136,21 @@
     @pl.when(jnp.logical_not(last))
     def _():
         prepare()
-
-    pl.semaphore_wait(barrier, jnp.where(last, 3, jnp.where(chip == chips - 2, 2 * peers - 1, peers + 1)))
-
-    for tk in range(2):
-        signal(back_x, below * 2 + tk, y)
-
-    halo = []
-
-    def send_rows(dq):
-        for p in range(PARTS):
-            for tk in range(2) if dq else (None,):
-                core = 1 - k if tk is None else tk
-                first = core * CH + p * PCH
-                copy = pltpu.make_async_remote_copy(
-                    src_ref=slide.at[pl.ds(first, PCH)],
-                    dst_ref=xbuf.at[(1 - dq) * 2 + k, pl.ds(p * PCH, PCH)],
-                    send_sem=send1.at[p, 2 if tk is None else (1 - dq) * 2 + tk],
-                    recv_sem=recv1.at[p, (1 - dq) * 2 + k],
-                    device_id=({1: below, 0: chip, -1: above}[dq] * 2 + core, y),
-                    device_id_type=MESH,
-                )
-                copy.start()
-                halo.append(copy)
-
-    send_rows(1)
+        from_above = jnp.where(chip == 0, 0, 2)
+        from_below = jnp.where(chip == chips - 2, peers, 2)
+        pl.semaphore_wait(barrier, peers - 1 + from_above + from_below)
+        send_rows(1)
+
+    @pl.when(chip >= chips - 2)
+    def _():
+        for tk in range(2):
+            signal(back_x, below * 2 + tk, y)
+
+    @pl.when(jnp.logical_or(last, chip == 0))
+    def _():
+        pl.semaphore_wait(back_x, 2)
+
     send_rows(0)
-
-    pl.semaphore_wait(back_x, 2)
     send_rows(-1)
 
     @pl.when(last)
@@ -195,25 +213,33 @@
     obuf[0] = result[:, :128]
     obuf[1] = result[:, 128:]
     depth = 2 * CH
-    targets = sorted(range(chans), key=lambda t: min(t, chans - t))
-    back = []
-    for t in targets:
-        copy = pltpu.make_async_remote_copy(
-            src_ref=obuf.at[:, pl.ds(t * depth, depth)],
+
+    def send_back(t, slot):
+        return pltpu.make_async_remote_copy(
+            src_ref=obuf.at[:, pl.ds(pl.multiple_of(t * depth, depth), depth)],
             dst_ref=out.at[:, y],
-            send_sem=send3.at[t],
+            send_sem=send3.at[slot],
             recv_sem=recv3.at[y],
             device_id=(row, t),
             device_id_type=MESH,
         )
-        pl.when(y != t)(copy.start)
-        back.append(copy)
+
+    pl.when(y > 0)(send_back(0, 0).start)
+    for d in far:
+        t = (y + d) % chans
+        pl.when(t > 0)(send_back(t, d).start)
     out[:, y] = obuf[:, pl.ds(pl.multiple_of(y * depth, depth), depth), :]
 
-    for copy in halo + exchange:
+    for p in range(PARTS):
+        for dq in (1, 0, -1):
+            for tk in range(2 if dq else 1):
+                row_copy(dq, p, tk).wait_send()
+    for copy in exchange:
         copy.wait_send()
-    for t, copy in zip(targets, back):
-        pl.when(y != t)(copy.wait_send)
+    pl.when(y > 0)(send_back(0, 0).wait_send)
+    for d in far:
+        t = (y + d) % chans
+        pl.when(t > 0)(send_back(t, d).wait_send)
     for d in range(1, chans):
         part = out.at[:, (y + d) % chans]
         pltpu.make_async_copy(part, part, recv3.at[(y + d) % chans]).wait()

time: 33.2 us -> 32.9 us (level)
  the two profiles are of different devices: /device:TPU:16 before, /device:TPU:8 now
where the time goes in v3:
time: 32.9 us; the launch traced here: 32.8 us
  Pallas kernels  31.2 us (95%)
  local copies, waits for them, and re-layouts  1.61 us (5%)
    pallas_call x1, Pallas kernels, shards(): pl.pallas_call(functools.partial(kernel, chips, chans), out_shape=jax.Sha...  31.2 us
    transpose x1, local copies, waits for them, and re-layouts, shards(): return jnp.transpose(got, (2, 1, 0, 3)).reshape(slide.shape)  1.61 us

profile of v3, /device:TPU:8, one launch (start us, length us, event | category | flops | bytes accessed | tf_op | source)
XLA Modules:
  0.0 32.8 jit_solution(1031984665837710549)
XLA Ops:
  0.0 31.2 %shard_map.46 = bf16[2,8,32,128]{3,2,1,0:T(8,128)(2,1)} custom-call(bf16[32,8,256]{2,1,0:T(8,128)(2,1)} %slide.1, f32[31,32,31]{2,1,0:T(8,128)} %bitcast.6, bf16[1024,256]{1,0:T(8,128)(2,1)} %w_in.1, bf16[256,1024]{1,0:T(8,128)(2,1)} %w_out.1), custom_call_target="tpu_custom_call" | custom-call | tf_op jit(solution)/shard_map/pallas_call | solution.py:257
  31.2 1.6 %copy.7 = bf16[32,8,2,128]{3,1,2,0:T(8,128)(2,1)} copy(bf16[32,8,2,128]{3,0,1,2:T(8,128)(2,1)} %bitcast.5) | data formatting | bytes 262144 | tf_op jit(solution)/shard_map/transpose | solution.py:285

commit v4 on v3

--- a/solution.py
+++ b/solution.py
@@ -15,12 +15,11 @@
 STEP = 5
 SPAN = 7
 CH = 16
-ROWS = 16
+ROWS = 8
 WIN = 48
-GROUPS = 2
-GCH = CH // GROUPS
 PARTS = 4
 PCH = CH // PARTS
+MERGE = 2
 
 
 def iota(shape, dim):
@@ -160,50 +159,63 @@
     far = sorted(range(1, chans), key=lambda d: -min(d, chans - d))
     own_copy.wait()
     zeros = jnp.zeros((256 - STEP * WIN, 256), BF16)
-    exchange = []
-    for g in range(GROUPS):
-        for p in range(g * PARTS // GROUPS, (g + 1) * PARTS // GROUPS):
-            for slot in (0, 1, 4, 5, 3 - k):
-                part = xbuf.at[slot, pl.ds(p * PCH, PCH)]
-                pltpu.make_async_copy(part, part, recv1.at[p, slot]).wait()
-            for c in range(p * PCH, (p + 1) * PCH):
-                x = jnp.concatenate([xbuf[j, c].astype(F32) for j in range(6)], axis=0)
-                cols = [x.astype(BF16)]
+
+    def take(slot, p):
+        part = xbuf.at[slot, pl.ds(p * PCH, PCH)]
+        pltpu.make_async_copy(part, part, recv1.at[p, slot]).wait()
+
+    def across(wave, d):
+        t = (y + d) % chans
+        return pltpu.make_async_remote_copy(
+            src_ref=sbuf.at[wave, t],
+            dst_ref=rbuf.at[m],
+            send_sem=send2.at[wave, d],
+            recv_sem=recv2.at[m],
+            device_id=(chip * 2 + wave, t),
+            device_id_type=MESH,
+        )
+
+    for wave in (1, 0):
+        for q in range(0, PARTS, MERGE):
+            for p in range(q, q + MERGE):
+                if wave == 1:
+                    for slot in (4, 5, 3 - k, 1):
+                        take(slot, p)
+                else:
+                    take(0, p)
+            for c in range(q * PCH, (q + MERGE) * PCH):
+                x = [xbuf[j, c] for j in range(wave, 6)]
+                total = x[2].astype(F32)
+                if wave == 1:
+                    x.append(jnp.zeros_like(x[0]))
+                cols = [jnp.concatenate(x, axis=0)]
                 for b in range(1, STEP):
                     cols.append(pltpu.roll(cols[0], 256 - b, 1))
                 prod = jnp.dot(toep[c], jnp.concatenate(cols + [zeros], axis=0), preferred_element_type=F32)
-                total = x[ROWS : 2 * ROWS]
                 for b in range(SPAN):
                     piece = prod[b * ROWS : (b + 1) * ROWS]
                     shift = (TAPS // 2 - STEP * b) % 256
                     total = total + (pltpu.roll(piece, shift, 1) if shift else piece)
-                mbuf[c] = total
-        mixed = mbuf[pl.ds(g * GCH, GCH)]
-        sbuf[g] = jnp.swapaxes(mixed, 0, 1).astype(BF16)
-        for d in far + [0]:
-            for tk in (0, 1) if d else (None,):
-                core = 1 - k if tk is None else tk
-                t = (y + d) % chans
-                copy = pltpu.make_async_remote_copy(
-                    src_ref=sbuf.at[g, core * chans + t],
-                    dst_ref=rbuf.at[g, m],
-                    send_sem=send2.at[g, 2 * d + (tk or 0)],
-                    recv_sem=recv2.at[g, m],
-                    device_id=(chip * 2 + core, t),
-                    device_id_type=MESH,
-                )
-                copy.start()
-                exchange.append(copy)
-        rbuf[g, m] = sbuf[g, k * chans + y]
+                mbuf[wave, c] = total
+        sbuf[wave] = jnp.swapaxes(mbuf[wave], 0, 1).astype(BF16)
+        for d in far:
+            across(wave, d).start()
+
+        @pl.when(k == wave)
+        def _():
+            rbuf[m] = sbuf[wave, y]
+
+        @pl.when(k != wave)
+        def _():
+            across(wave, 0).start()
 
     win_copy.wait()
     wout_copy.wait()
-    for g in range(GROUPS):
-        for d in range(1, peers):
-            part = rbuf.at[g, (m + d) % peers]
-            pltpu.make_async_copy(part, part, recv2.at[g, (m + d) % peers]).wait()
-    inner = jnp.concatenate([rbuf[g, s].astype(F32) for s in range(peers) for g in range(GROUPS)], axis=0)
-    flat = inner.astype(BF16)
+    for d in range(1, peers):
+        part = rbuf.at[(m + d) % peers]
+        pltpu.make_async_copy(part, part, recv2.at[(m + d) % peers]).wait()
+    inner = rbuf[...].reshape(256, 256).astype(F32)
+    flat = rbuf[...].reshape(256, 256)
     branch = jnp.zeros((256, 256), F32)
     for f in range(4):
         v = jnp.dot(win_v[pl.ds(f * 256, 256), :], flat, preferred_element_type=F32)
@@ -234,8 +246,10 @@
         for dq in (1, 0, -1):
             for tk in range(2 if dq else 1):
                 row_copy(dq, p, tk).wait_send()
-    for copy in exchange:
-        copy.wait_send()
+    for wave in (1, 0):
+        for d in far:
+            across(wave, d).wait_send()
+        pl.when(k != wave)(across(wave, 0).wait_send)
     pl.when(y > 0)(send_back(0, 0).wait_send)
     for d in far:
         t = (y + d) % chans
@@ -265,14 +279,14 @@
                 pltpu.VMEM((CH, SPAN * ROWS, 256), BF16),
                 pltpu.VMEM(w_in.shape, BF16),
                 pltpu.VMEM(w_out.shape, BF16),
-                pltpu.VMEM((CH, ROWS, width), F32),
-                pltpu.VMEM((GROUPS, ROWS, GCH, width), BF16),
-                pltpu.VMEM((GROUPS, peers, GCH, width), BF16),
+                pltpu.VMEM((2, CH, ROWS, width), F32),
+                pltpu.VMEM((2, ROWS, CH, width), BF16),
+                pltpu.VMEM((peers, CH, width), BF16),
                 pltpu.VMEM((2, 256, width // 2), BF16),
                 pltpu.SemaphoreType.DMA((PARTS, 6)),
                 pltpu.SemaphoreType.DMA((PARTS, 6)),
-                pltpu.SemaphoreType.DMA((GROUPS, peers)),
-                pltpu.SemaphoreType.DMA((GROUPS, peers)),
+                pltpu.SemaphoreType.DMA((2, chans)),
+                pltpu.SemaphoreType.DMA((peers,)),
                 pltpu.SemaphoreType.DMA((chans,)),
                 pltpu.SemaphoreType.DMA((chans,)),
                 pltpu.SemaphoreType.DMA((4,)),

time: 32.9 us -> 31.9 us (0.970)
  Pallas kernels: 31.2 us -> 30.1 us
    pallas_call x1, Pallas kernels: 31.2 us -> 30.1 us  [shards(): pl.pallas_call(functools.partial(kernel, chips, chans), out_shape=jax.Sha...]
where the time goes in v4:
time: 31.9 us; the launch traced here: 31.7 us
  Pallas kernels  30.1 us (94%)
  local copies, waits for them, and re-layouts  1.61 us (5%)
    pallas_call x1, Pallas kernels, shards(): pl.pallas_call(functools.partial(kernel, chips, chans), out_shape=jax.Sha...  30.1 us
    transpose x1, local copies, waits for them, and re-layouts, shards(): return jnp.transpose(got, (2, 1, 0, 3)).reshape(slide.shape)  1.61 us

profile of v4, /device:TPU:8, one launch (start us, length us, event | category | flops | bytes accessed | tf_op | source)
XLA Modules:
  0.0 31.7 jit_solution(12395904678804355635)
XLA Ops:
  0.0 30.1 %shard_map.46 = bf16[2,8,32,128]{3,2,1,0:T(8,128)(2,1)} custom-call(bf16[32,8,256]{2,1,0:T(8,128)(2,1)} %slide.1, f32[31,32,31]{2,1,0:T(8,128)} %bitcast.6, bf16[1024,256]{1,0:T(8,128)(2,1)} %w_in.1, bf16[256,1024]{1,0:T(8,128)(2,1)} %w_out.1), custom_call_target="tpu_custom_call" | custom-call | tf_op jit(solution)/shard_map/pallas_call | solution.py:271
  30.1 1.6 %copy.7 = bf16[32,8,2,128]{3,1,2,0:T(8,128)(2,1)} copy(bf16[32,8,2,128]{3,0,1,2:T(8,128)(2,1)} %bitcast.5) | data formatting | bytes 262144 | tf_op jit(solution)/shard_map/transpose | solution.py:299

commit v5 on v4

--- a/solution.py
+++ b/solution.py
@@ -17,9 +17,9 @@
 CH = 16
 ROWS = 8
 WIN = 48
-PARTS = 4
+PARTS = 2
 PCH = CH // PARTS
-MERGE = 2
+MERGE = 1
 
 
 def iota(shape, dim):
@@ -236,10 +236,11 @@
             device_id_type=MESH,
         )
 
-    pl.when(y > 0)(send_back(0, 0).start)
+    pl.when(jnp.logical_and(y > 0, k == 1))(send_back(0, 0).start)
     for d in far:
         t = (y + d) % chans
         pl.when(t > 0)(send_back(t, d).start)
+    pl.when(jnp.logical_and(y > 0, k == 0))(send_back(0, 0).start)
     out[:, y] = obuf[:, pl.ds(pl.multiple_of(y * depth, depth), depth), :]
 
     for p in range(PARTS):
@@ -270,7 +271,7 @@
         hbm = pl.BlockSpec(memory_space=pltpu.HBM)
         got = pl.pallas_call(
             functools.partial(kernel, chips, chans),
-            out_shape=jax.ShapeDtypeStruct((2, rows, depth, width // 2), BF16),
+            out_shape=pltpu.VMEM((2, rows, depth, width // 2), BF16),
             in_specs=[hbm] * 4,
             out_specs=pl.BlockSpec(memory_space=pltpu.VMEM),
             scratch_shapes=[

time: 31.9 us -> 29.7 us (0.931)
  Pallas kernels: 30.1 us -> 28.9 us
  local copies, waits for them, and re-layouts: 1.61 us -> 0.71 us
    pallas_call x1, Pallas kernels: 30.1 us -> 28.9 us  [shards(): pl.pallas_call(functools.partial(kernel, chips, chans), out_shape=pltpu.V...]
    transpose x1, local copies, waits for them, and re-layouts: 1.61 us -> 0.71 us  [shards(): return jnp.transpose(got, (2, 1, 0, 3)).reshape(slide.shape)]
where the time goes in v5:
time: 29.7 us; the launch traced here: 29.6 us
  Pallas kernels  28.9 us (97%)
  local copies, waits for them, and re-layouts  0.71 us (2%)
    pallas_call x1, Pallas kernels, shards(): pl.pallas_call(functools.partial(kernel, chips, chans), out_shape=pltpu.V...  28.9 us
    transpose x1, local copies, waits for them, and re-layouts, shards(): return jnp.transpose(got, (2, 1, 0, 3)).reshape(slide.shape)  0.71 us

profile of v5, /device:TPU:8, one launch (start us, length us, event | category | flops | bytes accessed | tf_op | source)
XLA Modules:
  0.0 29.6 jit_solution(383728725312223524)
XLA Ops:
  0.0 28.9 %shard_map.46 = bf16[2,8,32,128]{3,2,1,0:T(8,128)(2,1)S(1)} custom-call(bf16[32,8,256]{2,1,0:T(8,128)(2,1)} %slide.1, f32[31,32,31]{2,1,0:T(8,128)} %bitcast.6, bf16[1024,256]{1,0:T(8,128)(2,1)} %w_in.1, bf16[256,1024]{1,0:T(8,128)(2,1)} %w_out.1), custom_call_target="tpu_custom_call" | custom-call | tf_op jit(solution)/shard_map/pallas_call | solution.py:272
  28.9 0.7 %copy.7 = bf16[32,8,2,128]{3,1,2,0:T(8,128)(2,1)} copy(bf16[32,8,2,128]{3,0,1,2:T(8,128)(2,1)S(1)} %bitcast.5) | data formatting | bytes 262144 | tf_op jit(solution)/shard_map/transpose | solution.py:300

commit v6 on v5

--- a/solution.py
+++ b/solution.py
@@ -86,7 +86,7 @@
             for tk in range(2 if dq else 1):
                 row_copy(dq, p, tk).start()
 
-    @pl.when(last)
+    @pl.when(jnp.logical_and(last, k == 1))
     def _():
         pl.semaphore_wait(barrier, 2)
         send_rows(1)
@@ -113,6 +113,11 @@
     wout_copy = pltpu.make_async_copy(w_out, wout_v, loc.at[3])
     for copy in (taps_copy, own_copy, win_copy, wout_copy):
         copy.start()
+
+    @pl.when(jnp.logical_and(last, k == 0))
+    def _():
+        pl.semaphore_wait(barrier, 2)
+        send_rows(1)
 
     def prepare():
         taps_copy.wait()
@@ -139,6 +144,7 @@
         from_below = jnp.where(chip == chips - 2, peers, 2)
         pl.semaphore_wait(barrier, peers - 1 + from_above + from_below)
         send_rows(1)
+        send_rows(0)
 
     @pl.when(chip >= chips - 2)
     def _():
@@ -149,7 +155,7 @@
     def _():
         pl.semaphore_wait(back_x, 2)
 
-    send_rows(0)
+    pl.when(last)(lambda: send_rows(0))
     send_rows(-1)
 
     @pl.when(last)
@@ -228,7 +234,7 @@
 
     def send_back(t, slot):
         return pltpu.make_async_remote_copy(
-            src_ref=obuf.at[:, pl.ds(pl.multiple_of(t * depth, depth), depth)],
+            src_ref=obuf.at[:, pl.ds(t * depth, depth)],
             dst_ref=out.at[:, y],
             send_sem=send3.at[slot],
             recv_sem=recv3.at[y],
@@ -237,9 +243,9 @@
         )
 
     pl.when(jnp.logical_and(y > 0, k == 1))(send_back(0, 0).start)
-    for d in far:
-        t = (y + d) % chans
-        pl.when(t > 0)(send_back(t, d).start)
+    early = sorted(range(1, chans), key=lambda t: min(t, chans - t))
+    for t in early:
+        pl.when(y != t)(send_back(t, t).start)
     pl.when(jnp.logical_and(y > 0, k == 0))(send_back(0, 0).start)
     out[:, y] = obuf[:, pl.ds(pl.multiple_of(y * depth, depth), depth), :]
 
@@ -251,10 +257,8 @@
         for d in far:
             across(wave, d).wait_send()
         pl.when(k != wave)(across(wave, 0).wait_send)
-    pl.when(y > 0)(send_back(0, 0).wait_send)
-    for d in far:
-        t = (y + d) % chans
-        pl.when(t > 0)(send_back(t, d).wait_send)
+    for t in range(chans):
+        pl.when(y != t)(send_back(t, t).wait_send)
     for d in range(1, chans):
         part = out.at[:, (y + d) % chans]
         pltpu.make_async_copy(part, part, recv3.at[(y + d) % chans]).wait()

time: 29.7 us -> 29.5 us (level)
  the two profiles are of different devices: /device:TPU:8 before, /device:TPU:16 now
where the time goes in v6:
time: 29.5 us; the launch traced here: 29.4 us
  Pallas kernels  28.7 us (97%)
  local copies, waits for them, and re-layouts  0.71 us (2%)
    pallas_call x1, Pallas kernels, shards(): pl.pallas_call(functools.partial(kernel, chips, chans), out_shape=pltpu.V...  28.7 us
    transpose x1, local copies, waits for them, and re-layouts, shards(): return jnp.transpose(got, (2, 1, 0, 3)).reshape(slide.shape)  0.71 us

profile of v6, /device:TPU:16, one launch (start us, length us, event | category | flops | bytes accessed | tf_op | source)
XLA Modules:
  0.0 29.4 jit_solution(12437616607640022120)
XLA Ops:
  0.0 28.7 %shard_map.46 = bf16[2,8,32,128]{3,2,1,0:T(8,128)(2,1)S(1)} custom-call(bf16[32,8,256]{2,1,0:T(8,128)(2,1)} %slide.1, f32[31,32,31]{2,1,0:T(8,128)} %bitcast.6, bf16[1024,256]{1,0:T(8,128)(2,1)} %w_in.1, bf16[256,1024]{1,0:T(8,128)(2,1)} %w_out.1), custom_call_target="tpu_custom_call" | custom-call | tf_op jit(solution)/shard_map/pallas_call | solution.py:276
  28.7 0.7 %copy.7 = bf16[32,8,2,128]{3,1,2,0:T(8,128)(2,1)} copy(bf16[32,8,2,128]{3,0,1,2:T(8,128)(2,1)S(1)} %bitcast.5) | data formatting | bytes 262144 | tf_op jit(solution)/shard_map/transpose | solution.py:304

commit v7 on v6

--- a/solution.py
+++ b/solution.py
@@ -222,11 +222,9 @@
         pltpu.make_async_copy(part, part, recv2.at[(m + d) % peers]).wait()
     inner = rbuf[...].reshape(256, 256).astype(F32)
     flat = rbuf[...].reshape(256, 256)
-    branch = jnp.zeros((256, 256), F32)
-    for f in range(4):
-        v = jnp.dot(win_v[pl.ds(f * 256, 256), :], flat, preferred_element_type=F32)
-        hidden = (v * (1.0 + lax.erf(v * (0.5**0.5))) * 0.5).astype(BF16)
-        branch = branch + jnp.dot(wout_v[:, pl.ds(f * 256, 256)], hidden, preferred_element_type=F32)
+    v = jnp.dot(win_v[...], flat, preferred_element_type=F32)
+    hidden = (v * (1.0 + lax.erf(v * (0.5**0.5))) * 0.5).astype(BF16)
+    branch = jnp.dot(wout_v[...], hidden, preferred_element_type=F32)
     result = (inner + branch.astype(BF16).astype(F32)).astype(BF16)
     obuf[0] = result[:, :128]
     obuf[1] = result[:, 128:]

time: 29.5 us -> 29.5 us (level)
  no operation moved by 1% of the time
where the time goes in v7:
time: 29.5 us; the launch traced here: 29.3 us
  Pallas kernels  28.6 us (97%)
  local copies, waits for them, and re-layouts  0.71 us (2%)
    pallas_call x1, Pallas kernels, shards(): pl.pallas_call(functools.partial(kernel, chips, chans), out_shape=pltpu.V...  28.6 us
    transpose x1, local copies, waits for them, and re-layouts, shards(): return jnp.transpose(got, (2, 1, 0, 3)).reshape(slide.shape)  0.71 us

profile of v7, /device:TPU:16, one launch (start us, length us, event | category | flops | bytes accessed | tf_op | source)
XLA Modules:
  0.0 29.3 jit_solution(5062043276839993596)
XLA Ops:
  0.0 28.6 %shard_map.46 = bf16[2,8,32,128]{3,2,1,0:T(8,128)(2,1)S(1)} custom-call(bf16[32,8,256]{2,1,0:T(8,128)(2,1)} %slide.1, f32[31,32,31]{2,1,0:T(8,128)} %bitcast.6, bf16[1024,256]{1,0:T(8,128)(2,1)} %w_in.1, bf16[256,1024]{1,0:T(8,128)(2,1)} %w_out.1), custom_call_target="tpu_custom_call" | custom-call | tf_op jit(solution)/shard_map/pallas_call | solution.py:274
  28.6 0.7 %copy.7 = bf16[32,8,2,128]{3,1,2,0:T(8,128)(2,1)} copy(bf16[32,8,2,128]{3,0,1,2:T(8,128)(2,1)S(1)} %bitcast.5) | data formatting | bytes 262144 | tf_op jit(solution)/shard_map/transpose | solution.py:302

commit v8 on v7

--- a/solution.py
+++ b/solution.py
@@ -33,6 +33,7 @@
     taps,
     w_in,
     w_out,
+    final,
     out,
     xbuf,
     tbuf,
@@ -260,6 +261,9 @@
     for d in range(1, chans):
         part = out.at[:, (y + d) % chans]
         pltpu.make_async_copy(part, part, recv3.at[(y + d) % chans]).wait()
+    for half in range(2):
+        px = pl.ds(half * 128, 128)
+        final[:, :, px] = jnp.swapaxes(out[half].astype(F32), 0, 1).astype(BF16)
 
 
 def solution(mesh):
@@ -273,10 +277,11 @@
         hbm = pl.BlockSpec(memory_space=pltpu.HBM)
         got = pl.pallas_call(
             functools.partial(kernel, chips, chans),
-            out_shape=pltpu.VMEM((2, rows, depth, width // 2), BF16),
+            out_shape=pltpu.VMEM((depth, rows, width), BF16),
             in_specs=[hbm] * 4,
             out_specs=pl.BlockSpec(memory_space=pltpu.VMEM),
             scratch_shapes=[
+                pltpu.VMEM((2, rows, depth, width // 2), BF16),
                 pltpu.VMEM((6, CH, rows, width), BF16),
                 pltpu.VMEM((TAPS + 1, CH, TAPS), F32),
                 pltpu.VMEM((CH, SPAN * ROWS, 256), BF16),
@@ -299,6 +304,6 @@
                 collective_id=0, has_side_effects=True, vmem_limit_bytes=60 * 2**20
             ),
         )(slide, jnp.transpose(kernel_taps, (1, 0, 2)), w_in, w_out)
-        return jnp.transpose(got, (2, 1, 0, 3)).reshape(slide.shape)
+        return got
 
     return jax.shard_map(shards, mesh=mesh, in_specs=placed, out_specs=placed[0], check_vma=False)

time: 29.5 us -> 29.5 us (level)
    transpose x1 -> x0, local copies, waits for them, and re-layouts: 0.71 us -> none  [shards(): return jnp.transpose(got, (2, 1, 0, 3)).reshape(slide.shape)]
    unnamed x0 -> x1, local copies, waits for them, and re-layouts: none -> 0.66 us
where the time goes in v8:
time: 29.5 us; the launch traced here: 29.3 us
  Pallas kernels  28.7 us (97%)
  local copies, waits for them, and re-layouts  0.66 us (2%)
    pallas_call x1, Pallas kernels, shards(): pl.pallas_call(functools.partial(kernel, chips, chans), out_shape=pltpu.V...  28.7 us
    unnamed x1, local copies, waits for them, and re-layouts  0.66 us

profile of v8, /device:TPU:16, one launch (start us, length us, event | category | flops | bytes accessed | tf_op | source)
XLA Modules:
  0.0 29.3 jit_solution(2567078111749248066)
XLA Ops:
  0.0 28.7 %shard_map.46 = bf16[32,8,256]{2,1,0:T(8,128)(2,1)S(1)} custom-call(bf16[32,8,256]{2,1,0:T(8,128)(2,1)} %slide.1, f32[31,32,31]{2,1,0:T(8,128)} %bitcast.1, bf16[1024,256]{1,0:T(8,128)(2,1)} %w_in.1, bf16[256,1024]{1,0:T(8,128)(2,1)} %w_out.1), custom_call_target="tpu_custom_call" | custom-call | tf_op jit(solution)/shard_map/pallas_call | solution.py:278
  28.7 0.7 %copy.6 = bf16[32,8,256]{2,1,0:T(8,128)(2,1)} copy(bf16[32,8,256]{2,1,0:T(8,128)(2,1)S(1)} %shard_map.46) | data formatting | bytes 262144

commit v9 on v7

--- a/solution.py
+++ b/solution.py
@@ -204,8 +204,12 @@
                     total = total + (pltpu.roll(piece, shift, 1) if shift else piece)
                 mbuf[wave, c] = total
         sbuf[wave] = jnp.swapaxes(mbuf[wave], 0, 1).astype(BF16)
-        for d in far:
-            across(wave, d).start()
+        for odd in range(2):
+            for d in far:
+                if wave == 0:
+                    pl.when((y + d) % 2 == odd)(across(wave, d).start)
+                elif odd == 0:
+                    across(wave, d).start()
 
         @pl.when(k == wave)
         def _():

time: 29.5 us -> 29.4 us (level)
  the two profiles are of different devices: /device:TPU:16 before, /device:TPU:40 now
where the time goes in v9:
time: 29.4 us; the launch traced here: 29.3 us
  Pallas kernels  28.5 us (97%)
  local copies, waits for them, and re-layouts  0.71 us (2%)
    pallas_call x1, Pallas kernels, shards(): pl.pallas_call(functools.partial(kernel, chips, chans), out_shape=pltpu.V...  28.5 us
    transpose x1, local copies, waits for them, and re-layouts, shards(): return jnp.transpose(got, (2, 1, 0, 3)).reshape(slide.shape)  0.71 us

profile of v9, /device:TPU:40, one launch (start us, length us, event | category | flops | bytes accessed | tf_op | source)
XLA Modules:
  0.0 29.3 jit_solution(4658202167070978532)
XLA Ops:
  0.0 28.5 %shard_map.46 = bf16[2,8,32,128]{3,2,1,0:T(8,128)(2,1)S(1)} custom-call(bf16[32,8,256]{2,1,0:T(8,128)(2,1)} %slide.1, f32[31,32,31]{2,1,0:T(8,128)} %bitcast.6, bf16[1024,256]{1,0:T(8,128)(2,1)} %w_in.1, bf16[256,1024]{1,0:T(8,128)(2,1)} %w_out.1), custom_call_target="tpu_custom_call" | custom-call | tf_op jit(solution)/shard_map/pallas_call | solution.py:278
  28.5 0.7 %copy.7 = bf16[32,8,2,128]{3,1,2,0:T(8,128)(2,1)} copy(bf16[32,8,2,128]{3,0,1,2:T(8,128)(2,1)S(1)} %bitcast.5) | data formatting | bytes 262144 | tf_op jit(solution)/shard_map/transpose | solution.py:306
